TPU v7x, 512 devices: a whole 4x8x8 slice. The times are simulated.
512 devices in a mesh: wall: 16 (over x, y_hi, core), space: 32 (over y_lo, z).
Axes of the slice: x: 4, y: 8 (y_hi: 2, y_lo: 4; y = y_hi * 4 + y_lo), z: 8, core: 2. Of those that a mesh axis runs over, the one named last changes fastest.
Arguments:
- velocity: float32 [16, 2048, 1024], P('wall', 'space'), may hold values from -6 to 6
Outputs:
- correlation: float32 [16, 1, 2048, 1024], P('wall', None, 'space')
All inputs are finite; a program needn't handle non-finite values.
Results may differ from a plain program's by a relative error of at most 0.0003.
Values sent between devices are 32-bit elements; how exact they have to be, the bound alone decides.
A program may use at most 64 MiB of HBM per device.

v0:
```python
from functools import partial
import math

import jax
import jax.numpy as jnp
from jax import lax
from jax.sharding import PartitionSpec as P

HIGHEST = lax.Precision.HIGHEST


def from_behind(x, axis, by):
    size = lax.axis_size(axis)
    pairs = [(i, i + by) for i in range(size) if 0 <= i + by < size]
    return lax.ppermute(x, axis, pairs)


def phases(row_count, col_count, period):
    product = (
        jnp.arange(row_count, dtype=jnp.int32)[:, None]
        * jnp.arange(col_count, dtype=jnp.int32)[None, :]
        % period
    )
    angles = product.astype(jnp.float32) * (2.0 * math.pi / period)
    return (jnp.cos(angles), jnp.sin(angles))


def rotate(values, half_width):
    return jnp.concatenate([values[..., half_width:], -values[..., :half_width]], axis=-1)


def block_matrix(length, sign_factor):
    cosine_table, sine_table = phases(length, length, length)
    upper_rows = jnp.concatenate([cosine_table, -sign_factor * sine_table], axis=1)
    lower_rows = jnp.concatenate([sign_factor * sine_table, cosine_table], axis=1)
    return jnp.concatenate([upper_rows, lower_rows], axis=0)


def forward_depth(velocity):
    planes, local_rows, depth_cells = velocity.shape
    inner_len = depth_cells // 8
    blocks = velocity.reshape(planes, local_rows, 8, inner_len)
    cosine_eight, sine_eight = phases(8, 8, 8)
    real_part = jnp.einsum("pxbz,bk->pxkz", blocks, cosine_eight, precision=HIGHEST)
    imag_part = -jnp.einsum("pxbz,bk->pxkz", blocks, sine_eight, precision=HIGHEST)
    twist_cos, twist_sin = phases(8, inner_len, depth_cells)
    turned_real = real_part * twist_cos + imag_part * twist_sin
    turned_imag = imag_part * twist_cos - real_part * twist_sin
    stacked = jnp.stack([turned_real, turned_imag], axis=3)
    matrix = block_matrix(inner_len, 1.0).reshape(2, inner_len, 2, inner_len)
    result = jnp.einsum("pxkdz,dzej->pkjex", stacked, matrix, precision=HIGHEST)
    return result.reshape(planes, depth_cells, 2 * local_rows)


def forward_span(received, spread):
    item_count, mode_count, merged = received.shape
    row_count = merged // (2 * spread)
    grid_rows = spread * row_count
    grid_view = received.reshape(item_count, mode_count, spread, 2 * row_count)
    cosine_table, sine_table = phases(spread, spread, spread)
    section_one = jnp.einsum("qksm,st->qktm", grid_view, cosine_table, precision=HIGHEST)
    section_one = section_one + rotate(
        jnp.einsum("qksm,st->qktm", grid_view, sine_table, precision=HIGHEST), row_count
    )
    twist_cos, twist_sin = phases(spread, row_count, grid_rows)
    tiled_cos = jnp.concatenate([twist_cos, twist_cos], axis=1)
    tiled_sin = jnp.concatenate([twist_sin, twist_sin], axis=1)
    second = section_one * tiled_cos + rotate(section_one, row_count) * tiled_sin
    return jnp.einsum("qktm,mn->qktn", second, block_matrix(row_count, 1.0), precision=HIGHEST)


def cross_spectrum(spectra, partner, row_count):
    own_real = spectra[:, None, ..., :row_count]
    own_imag = spectra[:, None, ..., row_count:]
    far_real = partner[None, :, ..., :row_count]
    far_imag = partner[None, :, ..., row_count:]
    cross_real = own_real * far_real + own_imag * far_imag
    cross_imag = own_real * far_imag - own_imag * far_real
    return jnp.concatenate([cross_real, cross_imag], axis=-1)


def inverse_span(pair_spectra):
    spread = pair_spectra.shape[2]
    row_count = pair_spectra.shape[3] // 2
    grid_rows = spread * row_count
    section_one = jnp.einsum(
        "qksm,mn->qksn", pair_spectra, block_matrix(row_count, -1.0), precision=HIGHEST
    )
    twist_cos, twist_sin = phases(spread, row_count, grid_rows)
    tiled_cos = jnp.concatenate([twist_cos, twist_cos], axis=1)
    tiled_sin = jnp.concatenate([twist_sin, twist_sin], axis=1)
    second = section_one * tiled_cos - rotate(section_one, row_count) * tiled_sin
    cosine_table, sine_table = phases(spread, spread, spread)
    result = jnp.einsum("qksm,st->qktm", second, cosine_table, precision=HIGHEST)
    return result - rotate(
        jnp.einsum("qksm,st->qktm", second, sine_table, precision=HIGHEST), row_count
    )


def inverse_depth(received, row_count, scale_factor):
    item_count = received.shape[0]
    depth_cells = received.shape[1]
    inner_len = depth_cells // 8
    grid_view = received.reshape(item_count, 8, inner_len, 2, row_count)
    matrix = block_matrix(inner_len, -1.0).reshape(2, inner_len, 2, inner_len)
    section_one = jnp.einsum("qkjdx,djea->qkxea", grid_view, matrix, precision=HIGHEST)
    real_part = section_one[:, :, :, 0]
    imag_part = section_one[:, :, :, 1]
    twist_cos, twist_sin = phases(8, inner_len, depth_cells)
    twist_cos = twist_cos[:, None, :]
    twist_sin = twist_sin[:, None, :]
    turned_real = real_part * twist_cos - imag_part * twist_sin
    turned_imag = imag_part * twist_cos + real_part * twist_sin
    cosine_eight, sine_eight = phases(8, 8, 8)
    result = jnp.einsum("qkxa,kb->qxba", turned_real, cosine_eight, precision=HIGHEST)
    result = result - jnp.einsum("qkxa,kb->qxba", turned_imag, sine_eight, precision=HIGHEST)
    return result.reshape(item_count, row_count, depth_cells) * scale_factor


def local(velocity):
    spread = lax.axis_size("space")
    partner_gap = lax.axis_size("wall") // 2
    planes, row_count, depth_cells = velocity.shape
    grid_cells = row_count * spread * depth_cells
    depth_spectra = forward_depth(velocity)
    spectra = forward_span(
        lax.all_to_all(depth_spectra, "space", split_axis=1, concat_axis=2, tiled=True),
        spread=spread,
    )
    partner = from_behind(spectra, "wall", -partner_gap)
    formed = cross_spectrum(spectra, partner, row_count)
    mirrored = from_behind(formed, "wall", partner_gap)
    sign_row = jnp.concatenate(
        [jnp.ones((row_count,), jnp.float32), -jnp.ones((row_count,), jnp.float32)]
    )
    swapped = jnp.swapaxes(mirrored, 0, 1)
    flipped = swapped * sign_row
    cross_spectra = jnp.where(lax.axis_index("wall") < partner_gap, formed, flipped)
    pair_spectra = cross_spectra.reshape(
        planes * planes, cross_spectra.shape[2], cross_spectra.shape[3], cross_spectra.shape[4]
    )
    columns = inverse_span(pair_spectra)
    scale_factor = 1.0 / (grid_cells * math.sqrt(grid_cells))
    finish = partial(inverse_depth, row_count=row_count, scale_factor=scale_factor)
    fields = finish(lax.all_to_all(columns, "space", split_axis=2, concat_axis=1, tiled=True))
    return fields.reshape(planes, planes, row_count, depth_cells)


def solution(mesh):
    in_specs = (P("wall", "space", None),)
    out_specs = P("wall", None, "space", None)
    return jax.shard_map(local, mesh=mesh, in_specs=in_specs, out_specs=out_specs, check_vma=False)
```

profile of v0, /device:TPU:6, one launch (start us, length us, event | category | flops | bytes accessed | tf_op | source)
XLA Modules:
  0.0 99.9 jit_solution(9001649574407134528)
XLA Ops:
  0.1 0.3 broadcast_multiply_fusion
  0.3 0.3 fusion.58
  0.6 1.0 %copy.48 = f32[8,8,8,128]{3,2,1,0:T(8,128)S(1)} copy(f32[8,8,8,128]{3,1,2,0:T(8,128)} %bitcast.151) | data formatting | bytes 524288
  1.6 0.4 convolution_bitcast_fusion.7
  2.2 0.4 add_bitcast_fusion.1
  2.7 0.6 convolution_bitcast_fusion.6
  3.3 0.3 copy.30
  3.6 1.8 %copy.31 = f32[1,1024,128]{2,0,1:T(1,128)} copy(f32[1,1024,128]{1,0,2:T(1,128)S(1)} %bitcast.149) | data formatting | bytes 1048576 | tf_op jit(solution)/shard_map/reshape | solution.py:52
  5.4 13.7 %all-to-all-start = ((f32[1,1024,128]{2,0,1:T(1,128)}), f32[1,1024,128]{2,0,1:T(1,128)S(1)}, u32[]{:S(2)}, u32[]{:S(2)}) async-start(f32[1,1024,128]{2,0,1:T(1,128)} %copy.31), calls=%async_computation | async-start | bytes 1048576 | tf_op jit(solution)/shard_map/all_to_all | solution.py:127
  19.7 16.3 %all-to-all-done = f32[1,1024,128]{2,0,1:T(1,128)S(1)} async-done(((f32[1,1024,128]{2,0,1:T(1,128)}), f32[1,1024,128]{2,0,1:T(1,128)S(1)}, u32[]{:S(2)}, u32[]{:S(2)}) %all-to-all-start) | async-done | bytes 524320 | tf_op jit(solution)/shard_map/all_to_all | solution.py:127
  36.0 0.9 convolution_bitcast_fusion.4
  36.9 0.2 fusion.146
  37.1 0.9 fusion
  38.2 0.7 convolution_bitcast_fusion.3
  38.9 3.4 %collective-permute-start = (f32[1,32,32,128]{3,2,1,0:T(8,128)S(1)}, f32[1,32,32,128]{3,2,1,0:T(8,128)S(1)}, u32[]{:S(2)}, u32[]{:S(2)}) collective-permute-start(f32[1,32,32,128]{3,2,1,0:T(8,128)S(1)} %convolution_bitcast_fusion.3), channel_id=1, source_target_pairs={{256,0},{288,32},{320,64},{352,96},{384,128},{416,160},{448,192},{... | collective-permute-start | bytes 1572872 | tf_op jit(solution)/shard_map/ppermute | solution.py:15
  42.3 8.9 %collective-permute-done = f32[1,32,32,128]{3,2,1,0:T(8,128)S(1)} collective-permute-done((f32[1,32,32,128]{3,2,1,0:T(8,128)S(1)}, f32[1,32,32,128]{3,2,1,0:T(8,128)S(1)}, u32[]{:S(2)}, u32[]{:S(2)}) %collective-permute-start) | collective-permute-done | bytes 524320 | tf_op jit(solution)/shard_map/ppermute | solution.py:15
  51.2 0.3 add_bitcast_fusion
  51.7 1.3 %collective-permute-start.1 = (f32[1,1,32,32,128]{4,3,2,1,0:T(8,128)S(1)}, f32[1,1,32,32,128]{4,3,2,1,0:T(8,128)S(1)}, u32[]{:S(2)}, u32[]{:S(2)}) collective-permute-start(f32[1,1,32,32,128]{4,3,2,1,0:T(8,128)S(1)} %pad_maximum_fusion), channel_id=1, source_target_pairs={{0,256},{32,288},{64,320},{96,352},{128,384},{160,416},{192,448},{... | collective-permute-start | bytes 1572872 | tf_op jit(solution)/shard_map/ppermute | solution.py:15
  53.1 12.7 %collective-permute-done.1 = f32[1,1,32,32,128]{4,3,2,1,0:T(8,128)S(1)} collective-permute-done((f32[1,1,32,32,128]{4,3,2,1,0:T(8,128)S(1)}, f32[1,1,32,32,128]{4,3,2,1,0:T(8,128)S(1)}, u32[]{:S(2)}, u32[]{:S(2)}) %collective-permute-start.1) | collective-permute-done | bytes 524320 | tf_op jit(solution)/shard_map/ppermute | solution.py:15
  65.8 0.6 fusion.13
  66.4 0.2 slice_bitcast_fusion
  66.6 0.2 fusion.12
  66.9 0.7 convolution_bitcast_fusion.1
  67.8 0.7 fusion.1
  68.5 1.1 %copy.33 = f32[1,32,32,128]{3,1,0,2:T(8,128)} copy(f32[1,32,32,128]{3,2,1,0:T(8,128)S(1)} %fusion.1) | data formatting | bytes 1048576 | tf_op jit(solution)/shard_map/sub | solution.py:95
  69.6 10.2 %all-to-all-start.1 = ((f32[1,32,32,128]{3,1,0,2:T(8,128)}), f32[1,32,32,128]{3,1,0,2:T(8,128)S(1)}, u32[]{:S(2)}, u32[]{:S(2)}) async-start(f32[1,32,32,128]{3,1,0,2:T(8,128)} %copy.33), calls=%async_computation.1 | async-start | bytes 1048576 | tf_op jit(solution)/shard_map/all_to_all | solution.py:145
  80.0 15.6 %all-to-all-done.1 = f32[1,32,32,128]{3,1,0,2:T(8,128)S(1)} async-done(((f32[1,32,32,128]{3,1,0,2:T(8,128)}), f32[1,32,32,128]{3,1,0,2:T(8,128)S(1)}, u32[]{:S(2)}, u32[]{:S(2)}) %all-to-all-start.1) | async-done | bytes 524320 | tf_op jit(solution)/shard_map/all_to_all | solution.py:145
  95.6 0.6 reshape.318
  96.2 1.8 %convolution_bitcast_fusion = f32[1,8,64,2,128]{4,2,3,1,0:T(8,128)S(1)} fusion(f32[8,128,2,64,1]{3,2,1,0,4:T(2,128)S(1)} %bitcast.145, f32[2,128,2,128]{3,2,1,0:T(2,128)S(1)} %reshape.319), kind=kOutput, calls=%fused_computation | convolution fusion | flops 402653184 | bytes 1310720 | tf_op jit(solution)/shard_map/qkjdx,djea->qkxea/dot_general | solution.py:106
  98.1 0.5 fusion.29
  98.6 0.5 fusion.3
  99.1 0.7 mul.682
  (16 shorter events, 1.6 us)
Async XLA Ops:
  5.4 30.6 %all-to-all-start = ((f32[1,1024,128]{2,0,1:T(1,128)}), f32[1,1024,128]{2,0,1:T(1,128)S(1)}, u32[]{:S(2)}, u32[]{:S(2)}) async-start(f32[1,1024,128]{2,0,1:T(1,128)} %copy.31), calls=%async_computation | async-start | bytes 1048576 | tf_op jit(solution)/shard_map/all_to_all | solution.py:127
  38.9 12.3 %collective-permute-start = (f32[1,32,32,128]{3,2,1,0:T(8,128)S(1)}, f32[1,32,32,128]{3,2,1,0:T(8,128)S(1)}, u32[]{:S(2)}, u32[]{:S(2)}) collective-permute-start(f32[1,32,32,128]{3,2,1,0:T(8,128)S(1)} %convolution_bitcast_fusion.3), channel_id=1, source_target_pairs={{256,0},{288,32},{320,64},{352,96},{384,128},{416,160},{448,192},{... | collective-permute-start | bytes 1572872 | tf_op jit(solution)/shard_map/ppermute | solution.py:15
  51.7 14.0 %collective-permute-start.1 = (f32[1,1,32,32,128]{4,3,2,1,0:T(8,128)S(1)}, f32[1,1,32,32,128]{4,3,2,1,0:T(8,128)S(1)}, u32[]{:S(2)}, u32[]{:S(2)}) collective-permute-start(f32[1,1,32,32,128]{4,3,2,1,0:T(8,128)S(1)} %pad_maximum_fusion), channel_id=1, source_target_pairs={{0,256},{32,288},{64,320},{96,352},{128,384},{160,416},{192,448},{... | collective-permute-start | bytes 1572872 | tf_op jit(solution)/shard_map/ppermute | solution.py:15
  53.0 12.7 %copy-start = (f32[128]{0:T(128)S(1)}, f32[128]{0:T(128)}, u32[]{:S(2)}) copy-start(f32[128]{0:T(128)} %constant.129.clone.1) | copy-start | bytes 1540
  69.6 26.0 %all-to-all-start.1 = ((f32[1,32,32,128]{3,1,0,2:T(8,128)}), f32[1,32,32,128]{3,1,0,2:T(8,128)S(1)}, u32[]{:S(2)}, u32[]{:S(2)}) async-start(f32[1,32,32,128]{3,1,0,2:T(8,128)} %copy.33), calls=%async_computation.1 | async-start | bytes 1048576 | tf_op jit(solution)/shard_map/all_to_all | solution.py:145
where the time goes:
time: 100 us; the launch traced here: 99.9 us
  waiting for transfers between devices  53.5 us (54%)
  starting transfers between devices  28.6 us (29%)
  matrix products  8.76 us (9%)
  local copies, waits for them, and re-layouts  5.84 us (6%)
  other arithmetic  2.88 us (3%)
    ppermute x2, waiting for transfers between devices, from_behind(): return lax.ppermute(x, axis, pairs)  21.6 us
    all_to_all x1, waiting for transfers between devices, local(): lax.all_to_all(depth_spectra, 'space', split_axis=1, concat_axis=2, tiled...  16.3 us
    all_to_all x1, waiting for transfers between devices, local(): lax.all_to_all(columns, 'space', split_axis=2, concat_axis=1, tiled=True)  15.6 us
    all_to_all x1, starting transfers between devices, local(): lax.all_to_all(depth_spectra, 'space', split_axis=1, concat_axis=2, tiled...  13.7 us
    all_to_all x1, starting transfers between devices, local(): lax.all_to_all(columns, 'space', split_axis=2, concat_axis=1, tiled=True)  10.2 us
    ppermute x2, starting transfers between devices, from_behind(): return lax.ppermute(x, axis, pairs)  4.64 us
  transfers between devices with their start and end apart: 4, of which 4 were waited for; matrix products, arithmetic and copies ran while one was open for 1% of the time, Pallas kernels for 0%

commit v1 on v0

v1 whole, which is shorter than its diff:
```python
import math

import jax
import jax.numpy as jnp
import ml_dtypes
import numpy as np
from jax import lax
from jax.experimental import pallas as pl
from jax.experimental.pallas import tpu as pltpu
from jax.sharding import PartitionSpec as P

F32 = jnp.float32
BF16 = jnp.bfloat16
HALF = math.sqrt(0.5)

NX, NZ = 2048, 1024
SPREAD, ROWS = 32, 64
PEERS = 2 * SPREAD
TILE = 8


def split_table(table):
    high = table.astype(ml_dtypes.bfloat16)
    low = (table - high.astype(np.float64)).astype(ml_dtypes.bfloat16)
    return high, low


def mode_of(block, n):
    if block:
        return 8 * n + block
    return np.where(n < 64, 8 * n, 8 * (n - 64) + 4)


def slots():
    kb, dev, part, ka = np.meshgrid(np.arange(2), np.arange(16), np.arange(2), np.arange(4), indexing="ij")
    return dev * 8 + ka * 2 + kb, part


def span_forward_tables():
    n, part = slots()
    n, part = n[..., None], part[..., None]
    zi = np.arange(128)
    out = np.zeros((4, 2, 128, 256))
    for block in range(4):
        angle = 2 * np.pi * (mode_of(block, n) * zi % NZ) / NZ
        cos, sin = np.cos(angle), np.sin(angle)
        from_re = np.where(part == 0, cos, -sin)
        from_im = np.where(part == 0, sin, cos)
        if block == 0:
            alternate = np.where(zi % 2 == 0, 1.0, -1.0)
            from_re = np.where((n == 0) & (part == 1), alternate, from_re)
            first = np.where(n < 64, from_re, 0.0)
            second = np.where(n < 64, 0.0, from_re)
        else:
            first, second = from_re, from_im
        out[block] = np.concatenate([first, second], axis=-1).reshape(2, 128, 256)
    high, low = split_table(out)
    return np.concatenate([high, low], axis=2)


def span_inverse_tables():
    n, part = slots()
    n, part = n[..., None], part[..., None]
    zi = np.arange(128)
    scale = (NX * NZ) ** -1.5
    out = np.zeros((4, 256, 256))
    for block in range(4):
        angle = 2 * np.pi * (mode_of(block, n) * zi % NZ) / NZ
        cos, sin = np.cos(angle), np.sin(angle)
        to_re = 2 * np.where(part == 0, cos, -sin)
        to_im = 2 * np.where(part == 0, sin, cos)
        if block == 0:
            alternate = np.where(zi % 2 == 0, 1.0, -1.0)
            to_re = np.where(n == 0, np.where(part == 0, 1.0, alternate), to_re)
            first = np.where(n < 64, to_re, 0.0)
            second = np.where(n < 64, 0.0, to_re)
        else:
            first, second = to_re, to_im
        out[block] = np.concatenate([first, second], axis=-1).reshape(256, 256) * scale
    high, low = split_table(out)
    return np.stack([high, low], axis=1)


def stream_outer_forward():
    out = np.zeros((2, 160, SPREAD, 2, 4))
    t, s = np.arange(SPREAD)[:, None], np.arange(SPREAD)[None, :]
    cos, sin = np.cos(2 * np.pi * (t * s % 32) / 32), np.sin(2 * np.pi * (t * s % 32) / 32)
    for ka in range(4):
        rows = slice(32 * ka, 32 * ka + 32)
        out[0, rows, :, 0, ka] = cos
        out[0, rows, :, 1, ka] = sin
        out[1, rows, :, 0, ka] = -sin
        out[1, rows, :, 1, ka] = cos
    out[0, 128:, :, 0, 0] = cos
    out[0, 128:, :, 1, 0] = -sin
    out[1, 128:, :, 0, 0] = -sin
    out[1, 128:, :, 1, 0] = -cos
    return np.stack(split_table(out.reshape(320, 256)))


def stream_outer_inverse():
    out = np.zeros((SPREAD, 2, 4, 2, 4, SPREAD))
    s, t = np.arange(SPREAD)[:, None], np.arange(SPREAD)[None, :]
    cos, sin = np.cos(2 * np.pi * (t * s % 32) / 32), np.sin(2 * np.pi * (t * s % 32) / 32)
    for ka in range(4):
        out[:, 0, ka, 0, ka] = cos
        out[:, 0, ka, 1, ka] = -sin
        out[:, 1, ka, 0, ka] = sin
        out[:, 1, ka, 1, ka] = cos
    return np.stack(split_table(out.reshape(256, 256)))


def stream_inner(sign):
    out = np.zeros((2, 2, ROWS, 2, 2, ROWS))
    r, m = np.arange(ROWS)[:, None], np.arange(ROWS)[None, :]
    cos, sin = np.cos(2 * np.pi * (r * m % 64) / 64), sign * np.sin(2 * np.pi * (r * m % 64) / 64)
    for kb in range(2):
        out[0, kb, :, 0, kb] = cos
        out[1, kb, :, 0, kb] = -sin
        out[0, kb, :, 1, kb] = sin
        out[1, kb, :, 1, kb] = cos
    return np.stack(split_table(out.reshape(256, 256)))


def twist_tables():
    t = np.tile(np.arange(SPREAD), 5)[:, None]
    r = np.tile(np.arange(ROWS), 2)[None, :]
    angle = 2 * np.pi * (t * r) / NX
    return np.stack([np.cos(angle), np.sin(angle)]).astype(np.float32)


def split(x):
    high = x.astype(BF16)
    return high, (x - high.astype(F32)).astype(BF16)


def mul(a, b):
    return jnp.dot(a, b, preferred_element_type=F32)


def mul_nt(a, b):
    return lax.dot_general(a, b, (((1,), (1,)), ((), ())), preferred_element_type=F32)


def kernel(
    u_hbm, wf_hbm, k1_hbm, d1_hbm, tw_hbm, d2_hbm, k2_hbm, wi_hbm, out_ref,
    u, wf, k1, d1, tw, d2, k2, wi, e_high, e_low, send1, recv1, send2, recv2,
    load_sem, send_sem, recv_sem,
):
    wall, space = lax.axis_index("wall"), lax.axis_index("space")
    pairs = lax.axis_size("wall") // 2
    plane = wall // pairs
    base = lax.rem(wall, pairs)
    y, z = space // 8, lax.rem(space, 8)
    me_mode = y * 16 + plane * 8 + z
    me_row = plane * SPREAD + space

    loads = []
    for i, (src, dst) in enumerate(
        [(u_hbm, u), (wf_hbm, wf), (k1_hbm, k1), (d1_hbm, d1), (tw_hbm, tw), (d2_hbm, d2), (k2_hbm, k2), (wi_hbm, wi)]
    ):
        loads.append(pltpu.make_async_copy(src, dst, load_sem.at[i]))
        loads[-1].start()

    barrier = pltpu.get_barrier_semaphore()

    def greet(i, carry):
        other = lax.rem(me_row + i, PEERS)
        pl.semaphore_signal(
            barrier, inc=1, device_id={"wall": base + pairs * (other // SPREAD), "space": lax.rem(other, SPREAD)},
            device_id_type=pl.DeviceIdType.MESH,
        )
        return carry

    lax.fori_loop(1, PEERS, greet, 0)

    def tile(ref, index):
        return ref.at[pl.ds(pl.multiple_of(index * TILE, TILE), TILE)]

    def send(stage, src, dst, to_plane, to_space):
        return pltpu.make_async_remote_copy(
            src_ref=src, dst_ref=dst, send_sem=send_sem.at[stage], recv_sem=recv_sem.at[stage],
            device_id={"wall": base + pairs * to_plane, "space": to_space},
            device_id_type=pl.DeviceIdType.MESH,
        )

    loads[0].wait()
    parts = [u[0, :, 128 * b : 128 * b + 128] for b in range(8)]
    plus = [parts[b] + parts[b + 4] for b in range(4)]
    minus = [parts[b] - parts[b + 4] for b in range(4)]
    even, odd = plus[0] + plus[2], plus[1] + plus[3]
    across, along = (minus[1] - minus[3]) * HALF, (minus[1] + minus[3]) * HALF
    eighths = [
        (even + odd, even - odd),
        (minus[0] + across, -minus[2] - along),
        (plus[0] - plus[2], plus[3] - plus[1]),
        (minus[0] - across, minus[2] - along),
    ]
    for block, (first, second) in enumerate(eighths):
        for half, value in enumerate((first, second)):
            high, low = split(value)
            e_high[block, :, 128 * half : 128 * half + 128] = high
            e_low[block, :, 128 * half : 128 * half + 128] = low

    loads[1].wait()
    nothing = jnp.zeros((ROWS, 256), BF16)
    for step in range(4):
        block = lax.rem(y + 2 + step, 4)
        high, low = e_high[block], e_low[block]
        both = mul_nt(wf[block, 0], jnp.concatenate([high, nothing, low, nothing], axis=0))
        both += mul_nt(wf[block, 1], jnp.concatenate([nothing, high, nothing, low], axis=0))
        send1[pl.ds(pl.multiple_of(block * 128, 128), 128), :] = both[:128, :128] + both[:128, 128:] + both[128:, :128]
        if step == 0:
            pl.semaphore_wait(barrier, PEERS - 1)

        def send_block(j, carry):
            to_plane = lax.rem(plane + 1 + j // 8, 2)
            to_z = lax.rem(z + 4 + j, 8)
            to = block * 16 + to_plane * 8 + to_z

            @pl.when(to != me_mode)
            def _():
                send(0, tile(send1, to), tile(recv1, me_row), to_plane, block * 8 + to_z).start()

            return carry

        lax.fori_loop(0, 16, send_block, 0)
    own1 = pltpu.make_async_copy(tile(send1, me_mode), tile(recv1, me_row), recv_sem.at[0])
    own1.start()
    for load in loads[2:]:
        load.wait()
    pltpu.make_async_copy(recv1, recv1, recv_sem.at[0]).wait()

    high, low = split(recv1[...])
    h = [high[:256], high[256:]]
    l = [low[:256], low[256:]]
    outer = mul(k1[0], jnp.concatenate([h[0], l[0], h[1], l[1]], axis=1))
    outer_low = mul(k1[1], jnp.concatenate(h, axis=1))
    cos, sin = tw[0], tw[1]
    turned = []
    for p in range(2):
        got = outer[:, 256 * p : 256 * p + 128] + outer[:, 256 * p + 128 : 256 * p + 256] + outer_low[:, 128 * p : 128 * p + 128]
        re, im = got[:160], got[160:]
        turned.append(jnp.concatenate([re * cos + im * sin, im * cos - re * sin], axis=1))
    high, low = split(jnp.concatenate(turned, axis=0))
    both = mul(jnp.concatenate([high, low], axis=0), d1[0])
    spectra = both[:320] + both[320:] + mul(high, d1[1])

    a_re, a_im = spectra[:128, :128], spectra[:128, 128:]
    b_re, b_im = spectra[160:288, :128], spectra[160:288, 128:]
    cross_re = a_re * b_re + a_im * b_im
    cross_im = a_re * b_im - a_im * b_re

    def unpack(column, mirror):
        c_re, c_im = column[:, :128], column[:, 128:]
        m_re, m_im = mirror[:, :128], mirror[:, 128:]
        return (c_re + m_re) * 0.5, (c_im + m_im) * 0.5, (c_im - m_im) * 0.5, (m_re - c_re) * 0.5

    a0_re, a0_im, a1_re, a1_im = unpack(spectra[:32], spectra[128:160])
    b0_re, b0_im, b1_re, b1_im = unpack(spectra[160:192], spectra[288:320])
    zero_re, zero_im = a0_re * b0_re + a0_im * b0_im, a0_re * b0_im - a0_im * b0_re
    last_re, last_im = a1_re * b1_re + a1_im * b1_im, a1_re * b1_im - a1_im * b1_re
    lane = lax.broadcasted_iota(jnp.int32, (32, 128), 1)
    packed = jnp.logical_and(lane < ROWS, me_mode == 0)

    def merge(special, plain):
        return jnp.concatenate([jnp.where(packed, special, plain[:32]), plain[32:]], axis=0)

    first = jnp.concatenate([merge(zero_re - last_im, cross_re), merge(zero_im + last_re, cross_im)], axis=1)
    second = jnp.concatenate([merge(zero_re + last_im, cross_re), merge(last_re - zero_im, -cross_im)], axis=1)

    high, low = split(jnp.concatenate([first, second], axis=0))
    both = mul(jnp.concatenate([high, low], axis=0), d2[0])
    inner = both[:256] + both[256:] + mul(high, d2[1])
    cos, sin = cos[:128], sin[:128]
    columns, columns_high = [], []
    for p in range(2):
        re, im = inner[128 * p : 128 * p + 128, :128], inner[128 * p : 128 * p + 128, 128:]
        high, low = split(jnp.concatenate([re * cos - im * sin, im * cos + re * sin], axis=0))
        columns += [high, low]
        columns_high.append(high)
    outer = mul(k2[0], jnp.concatenate(columns, axis=1))
    outer_low = mul(k2[1], jnp.concatenate(columns_high, axis=1))
    for p in range(2):
        send2[256 * p : 256 * p + 256, :] = (
            outer[:, 256 * p : 256 * p + 128] + outer[:, 256 * p + 128 : 256 * p + 256] + outer_low[:, 128 * p : 128 * p + 128]
        )

    def send_back(j, carry):
        to_plane = lax.rem(plane + 1 + j // SPREAD, 2)
        to_y = lax.rem(y + 2 + lax.rem(j, SPREAD) // 8, 4)
        to_z = lax.rem(z + 4 + j, 8)
        to_space = to_y * 8 + to_z
        to = to_plane * SPREAD + to_space

        @pl.when(to != me_row)
        def _():
            send(1, tile(send2, to), tile(recv2, me_mode), to_plane, to_space).start()

        return carry

    lax.fori_loop(0, PEERS, send_back, 0)
    own2 = pltpu.make_async_copy(tile(send2, me_row), tile(recv2, me_mode), recv_sem.at[1])
    own2.start()
    pltpu.make_async_copy(recv2, recv2, recv_sem.at[1]).wait()

    fields = []
    for block in range(4):
        flat = recv2[128 * block : 128 * block + 128, :].T
        high, low = split(jnp.concatenate([flat[:ROWS], flat[ROWS:]], axis=1))
        both = mul(jnp.concatenate([high, low], axis=0), wi[block, 0])
        fields.append(both[:ROWS] + both[ROWS:] + mul(high, wi[block, 1]))
    (h0, h4), (r1, i1), (r2, i2), (r3, i3) = [(f[:, :128], f[:, 128:]) for f in fields]
    sums, differences = h0 + h4, h0 - h4
    evens = [sums + r2, differences - i2, sums - r2, differences + i2]
    odds = [r1 + r3, (r1 - r3 - i1 - i3) * HALF, i3 - i1, (r3 - r1 - i1 - i3) * HALF]
    for b in range(4):
        out_ref[0, 0, :, 128 * b : 128 * b + 128] = evens[b] + odds[b]
        out_ref[0, 0, :, 128 * b + 512 : 128 * b + 640] = evens[b] - odds[b]

    count = (PEERS - 1) * TILE
    for stage, buffer in enumerate((send1, send2)):
        pltpu.make_async_copy(buffer.at[pl.ds(0, count)], buffer.at[pl.ds(0, count)], send_sem.at[stage]).wait()


def local(velocity):
    tables = [
        span_forward_tables(), stream_outer_forward(), stream_inner(-1.0), twist_tables(),
        stream_inner(1.0), stream_outer_inverse(), span_inverse_tables(),
    ]
    tables = [jnp.asarray(t) for t in tables]
    messages = pltpu.VMEM((PEERS * TILE, 128), F32)
    return pl.pallas_call(
        kernel,
        out_shape=jax.ShapeDtypeStruct((1, 1, ROWS, NZ), F32),
        in_specs=[pl.BlockSpec(memory_space=pl.ANY)] * 8,
        out_specs=pl.BlockSpec(memory_space=pltpu.VMEM),
        scratch_shapes=[pltpu.VMEM(velocity.shape, F32)]
        + [pltpu.VMEM(t.shape, t.dtype) for t in tables]
        + [pltpu.VMEM((4, ROWS, 256), BF16)] * 2
        + [messages] * 4
        + [pltpu.SemaphoreType.DMA((8,)), pltpu.SemaphoreType.DMA((2,)), pltpu.SemaphoreType.DMA((2,))],
        compiler_params=pltpu.CompilerParams(
            collective_id=0, has_side_effects=True, vmem_limit_bytes=32 * 1024 * 1024
        ),
    )(velocity, *tables)


def solution(mesh):
    return jax.shard_map(
        local, mesh=mesh, in_specs=(P("wall", "space", None),), out_specs=P("wall", None, "space", None), check_vma=False
    )
```

time: 100 us -> 46.5 us (0.47)
  the two profiles are of different devices: /device:TPU:6 before, /device:TPU:56 now
where the time goes in v1:
time: 46.5 us; the launch traced here: 46.1 us
  Pallas kernels  37.3 us (80%)
  local copies, waits for them, and re-layouts  8.84 us (19%)
    pallas_call x1, Pallas kernels, local(): pl.pallas_call(kernel, out_shape=jax.ShapeDtypeStruct((1, 1, ROWS, NZ), F...  37.3 us
    unnamed x17, local copies, waits for them, and re-layouts  8.84 us

profile of v1, /device:TPU:56, one launch (start us, length us, event | category | flops | bytes accessed | tf_op | source)
XLA Modules:
  0.0 46.1 jit_solution(6803097917448471056)
XLA Ops:
  0.0 0.0 copy-start
  0.0 1.2 %copy-done = bf16[4,2,256,256]{3,2,1,0:T(8,128)(2,1)S(1)} copy-done((bf16[4,2,256,256]{3,2,1,0:T(8,128)(2,1)S(1)}, bf16[4,2,256,256]{3,2,1,0:T(8,128)(2,1)}, u32[]{:S(2)}) %copy-start) | copy-done | bytes 1048600
  1.2 0.0 copy-start.1
  1.2 1.2 %copy-done.1 = bf16[4,2,256,256]{3,2,1,0:T(8,128)(2,1)S(1)} copy-done((bf16[4,2,256,256]{3,2,1,0:T(8,128)(2,1)S(1)}, bf16[4,2,256,256]{3,2,1,0:T(8,128)(2,1)}, u32[]{:S(2)}) %copy-start.1) | copy-done | bytes 1048600
  2.5 0.0 copy-start.2
  2.5 1.0 %copy-done.2 = bf16[2,320,256]{2,1,0:T(8,128)(2,1)S(1)} copy-done((bf16[2,320,256]{2,1,0:T(8,128)(2,1)S(1)}, bf16[2,320,256]{2,1,0:T(8,128)(2,1)}, u32[]{:S(2)}) %copy-start.2) | copy-done | bytes 327704
  3.4 0.0 copy-start.3
  3.4 0.9 %copy-done.3 = f32[1,64,1024]{2,1,0:T(8,128)S(1)} copy-done((f32[1,64,1024]{2,1,0:T(8,128)S(1)}, f32[1,64,1024]{2,1,0:T(8,128)}, u32[]{:S(2)}) %copy-start.3) | copy-done | bytes 262168
  4.4 0.0 copy-start.4
  4.4 0.9 %copy-done.4 = bf16[2,256,256]{2,1,0:T(8,128)(2,1)S(1)} copy-done((bf16[2,256,256]{2,1,0:T(8,128)(2,1)S(1)}, bf16[2,256,256]{2,1,0:T(8,128)(2,1)}, u32[]{:S(2)}) %copy-start.4) | copy-done | bytes 262168
  5.3 0.0 copy-start.5
  5.3 0.9 %copy-done.5 = bf16[2,256,256]{2,1,0:T(8,128)(2,1)S(1)} copy-done((bf16[2,256,256]{2,1,0:T(8,128)(2,1)S(1)}, bf16[2,256,256]{2,1,0:T(8,128)(2,1)}, u32[]{:S(2)}) %copy-start.5) | copy-done | bytes 262168
  6.3 0.0 copy-start.6
  6.3 0.9 %copy-done.6 = bf16[2,256,256]{2,1,0:T(8,128)(2,1)S(1)} copy-done((bf16[2,256,256]{2,1,0:T(8,128)(2,1)S(1)}, bf16[2,256,256]{2,1,0:T(8,128)(2,1)}, u32[]{:S(2)}) %copy-start.6) | copy-done | bytes 262168
  7.2 0.0 copy-start.7
  7.2 0.9 %copy-done.7 = f32[2,160,128]{2,1,0:T(8,128)S(1)} copy-done((f32[2,160,128]{2,1,0:T(8,128)S(1)}, f32[2,160,128]{2,1,0:T(8,128)}, u32[]{:S(2)}) %copy-start.7) | copy-done | bytes 163864
  8.1 37.3 %shard_map.82 = f32[1,1,64,1024]{3,2,1,0:T(8,128)S(1)} custom-call(f32[1,64,1024]{2,1,0:T(8,128)S(1)} %copy-done.3, bf16[4,2,256,256]{3,2,1,0:T(8,128)(2,1)S(1)} %copy-done.1, bf16[2,320,256]{2,1,0:T(8,128)(2,1)S(1)} %copy-done.2, bf16[2,256,256]{2,1,0:T(8,128)(2,1)S(1)} %copy-done.6, f32[2,160,128]{2,1,0:T(8,128)S(1)} %copy-done.7, ...), custom_call_target="tpu_custom_call" | custom-call | tf_op jit(solution)/shard_map/pallas_call | solution.py:333
  45.4 0.7 %copy.10 = f32[1,1,64,1024]{3,2,1,0:T(8,128)} copy(f32[1,1,64,1024]{3,2,1,0:T(8,128)S(1)} %shard_map.82) | data formatting | bytes 524288
Async XLA Ops:
  0.0 1.2 %copy-start = (bf16[4,2,256,256]{3,2,1,0:T(8,128)(2,1)S(1)}, bf16[4,2,256,256]{3,2,1,0:T(8,128)(2,1)}, u32[]{:S(2)}) copy-start(bf16[4,2,256,256]{3,2,1,0:T(8,128)(2,1)} %constant.20.clone.wi_hbm) | copy-start | bytes 3145732
  1.2 1.2 %copy-start.1 = (bf16[4,2,256,256]{3,2,1,0:T(8,128)(2,1)S(1)}, bf16[4,2,256,256]{3,2,1,0:T(8,128)(2,1)}, u32[]{:S(2)}) copy-start(bf16[4,2,256,256]{3,2,1,0:T(8,128)(2,1)} %constant.14.clone.wf_hbm) | copy-start | bytes 3145732
  2.5 1.0 %copy-start.2 = (bf16[2,320,256]{2,1,0:T(8,128)(2,1)S(1)}, bf16[2,320,256]{2,1,0:T(8,128)(2,1)}, u32[]{:S(2)}) copy-start(bf16[2,320,256]{2,1,0:T(8,128)(2,1)} %constant.15.clone.k1_hbm) | copy-start | bytes 983044
  3.4 0.9 %copy-start.3 = (f32[1,64,1024]{2,1,0:T(8,128)S(1)}, f32[1,64,1024]{2,1,0:T(8,128)}, u32[]{:S(2)}) copy-start(f32[1,64,1024]{2,1,0:T(8,128)} %u_hbm.1) | copy-start | bytes 786436
  4.4 0.9 %copy-start.4 = (bf16[2,256,256]{2,1,0:T(8,128)(2,1)S(1)}, bf16[2,256,256]{2,1,0:T(8,128)(2,1)}, u32[]{:S(2)}) copy-start(bf16[2,256,256]{2,1,0:T(8,128)(2,1)} %constant.19.clone.k2_hbm) | copy-start | bytes 786436
  5.3 0.9 %copy-start.5 = (bf16[2,256,256]{2,1,0:T(8,128)(2,1)S(1)}, bf16[2,256,256]{2,1,0:T(8,128)(2,1)}, u32[]{:S(2)}) copy-start(bf16[2,256,256]{2,1,0:T(8,128)(2,1)} %constant.18.clone.d2_hbm) | copy-start | bytes 786436
  6.3 0.9 %copy-start.6 = (bf16[2,256,256]{2,1,0:T(8,128)(2,1)S(1)}, bf16[2,256,256]{2,1,0:T(8,128)(2,1)}, u32[]{:S(2)}) copy-start(bf16[2,256,256]{2,1,0:T(8,128)(2,1)} %constant.16.clone.d1_hbm) | copy-start | bytes 786436
  7.2 0.9 %copy-start.7 = (f32[2,160,128]{2,1,0:T(8,128)S(1)}, f32[2,160,128]{2,1,0:T(8,128)}, u32[]{:S(2)}) copy-start(f32[2,160,128]{2,1,0:T(8,128)} %constant.17.clone.tw_hbm) | copy-start | bytes 491524

commit v2 on v1

v2 whole, which is shorter than its diff:
```python
import math

import jax
import jax.numpy as jnp
import ml_dtypes
import numpy as np
from jax import lax
from jax.experimental import pallas as pl
from jax.experimental.pallas import tpu as pltpu
from jax.sharding import PartitionSpec as P

F32 = jnp.float32
BF16 = jnp.bfloat16
HALF = math.sqrt(0.5)

NX, NZ = 2048, 1024
SPREAD, ROWS = 32, 64
PEERS = 2 * SPREAD
TILE = 8


def split_table(table):
    high = table.astype(ml_dtypes.bfloat16)
    low = (table - high.astype(np.float64)).astype(ml_dtypes.bfloat16)
    return high, low


def mode_of(block, n):
    if block:
        return 8 * n + block
    return np.where(n < 64, 8 * n, 8 * (n - 64) + 4)


def slots():
    kb, dev, chunk, part, ka = np.meshgrid(*map(np.arange, (2, 16, 2, 2, 2)), indexing="ij")
    return dev * 8 + chunk * 4 + ka * 2 + kb, part


def span_forward_tables():
    n, part = slots()
    n, part = n[..., None], part[..., None]
    zi = np.arange(128)
    out = np.zeros((4, 2, 128, 256))
    for block in range(4):
        angle = 2 * np.pi * (mode_of(block, n) * zi % NZ) / NZ
        cos, sin = np.cos(angle), np.sin(angle)
        from_re = np.where(part == 0, cos, -sin)
        from_im = np.where(part == 0, sin, cos)
        if block == 0:
            alternate = np.where(zi % 2 == 0, 1.0, -1.0)
            from_re = np.where((n == 0) & (part == 1), alternate, from_re)
            first = np.where(n < 64, from_re, 0.0)
            second = np.where(n < 64, 0.0, from_re)
        else:
            first, second = from_re, from_im
        out[block] = np.concatenate([first, second], axis=-1).reshape(2, 128, 256)
    high, low = split_table(out)
    return np.concatenate([high, low], axis=2)


def span_inverse_tables():
    n, part = slots()
    n, part = n[..., None], part[..., None]
    zi = np.arange(128)
    scale = (NX * NZ) ** -1.5
    out = np.zeros((4, 256, 256))
    for block in range(4):
        angle = 2 * np.pi * (mode_of(block, n) * zi % NZ) / NZ
        cos, sin = np.cos(angle), np.sin(angle)
        to_re = 2 * np.where(part == 0, cos, -sin)
        to_im = 2 * np.where(part == 0, sin, cos)
        if block == 0:
            alternate = np.where(zi % 2 == 0, 1.0, -1.0)
            to_re = np.where(n == 0, np.where(part == 0, 1.0, alternate), to_re)
            first = np.where(n < 64, to_re, 0.0)
            second = np.where(n < 64, 0.0, to_re)
        else:
            first, second = to_re, to_im
        out[block] = np.concatenate([first, second], axis=-1).reshape(256, 256) * scale
    high, low = split_table(out)
    return np.stack([high, low], axis=1)


def stream_outer_forward():
    out = np.zeros((2, 96, SPREAD, 8))
    t, s = np.arange(SPREAD)[:, None], np.arange(SPREAD)[None, :]
    cos, sin = np.cos(2 * np.pi * (t * s % 32) / 32), np.sin(2 * np.pi * (t * s % 32) / 32)
    for ka in range(2):
        rows = slice(32 * ka, 32 * ka + 32)
        out[0, rows, :, ka] = cos
        out[0, rows, :, 2 + ka] = sin
        out[1, rows, :, ka] = -sin
        out[1, rows, :, 2 + ka] = cos
    out[0, 64:, :, 0] = cos
    out[0, 64:, :, 2] = -sin
    out[1, 64:, :, 0] = -sin
    out[1, 64:, :, 2] = -cos
    return np.stack(split_table(out.reshape(192, 256)))


def stream_outer_inverse():
    out = np.zeros((SPREAD, 2, 2, 2, 2, SPREAD))
    s, t = np.arange(SPREAD)[:, None], np.arange(SPREAD)[None, :]
    cos, sin = np.cos(2 * np.pi * (t * s % 32) / 32), np.sin(2 * np.pi * (t * s % 32) / 32)
    for ka in range(2):
        out[:, 0, ka, 0, ka] = cos
        out[:, 0, ka, 1, ka] = -sin
        out[:, 1, ka, 0, ka] = sin
        out[:, 1, ka, 1, ka] = cos
    return np.stack(split_table(out.reshape(128, 128)))


def stream_inner(sign):
    out = np.zeros((2, 2, ROWS, 2, 2, ROWS))
    r, m = np.arange(ROWS)[:, None], np.arange(ROWS)[None, :]
    cos, sin = np.cos(2 * np.pi * (r * m % 64) / 64), sign * np.sin(2 * np.pi * (r * m % 64) / 64)
    for kb in range(2):
        out[0, kb, :, 0, kb] = cos
        out[1, kb, :, 0, kb] = -sin
        out[0, kb, :, 1, kb] = sin
        out[1, kb, :, 1, kb] = cos
    return np.stack(split_table(out.reshape(256, 256)))


def twist_tables():
    t = np.tile(np.arange(SPREAD), 3)[:, None]
    r = np.tile(np.arange(ROWS), 2)[None, :]
    angle = 2 * np.pi * (t * r) / NX
    return np.stack([np.cos(angle), np.sin(angle)]).astype(np.float32)


def split(x):
    high = x.astype(BF16)
    return high, (x - high.astype(F32)).astype(BF16)


def mul(a, b):
    return jnp.dot(a, b, preferred_element_type=F32)


def mul_nt(a, b):
    return lax.dot_general(a, b, (((1,), (1,)), ((), ())), preferred_element_type=F32)


def stream_chunk(chunk, recv1, send2, k1, d1, d2, k2, cos, sin, used, me_mode):
    halves = [split(jnp.where(used, recv1[chunk, 256 * p : 256 * p + 256, :], 0.0)) for p in range(2)]
    extra = 32 if chunk == 0 else 0
    rows = 64 + extra

    def table(part):
        return k1[part] if chunk == 0 else jnp.concatenate([k1[part, :64], k1[part, 96:160]], axis=0)

    outer = mul(table(0), jnp.concatenate([x for pair in halves for x in pair], axis=1))
    outer_low = mul(table(1), jnp.concatenate([high for high, _ in halves], axis=1))
    turned = []
    for p in range(2):
        got = outer[:, 256 * p : 256 * p + 128] + outer[:, 256 * p + 128 : 256 * p + 256] + outer_low[:, 128 * p : 128 * p + 128]
        re, im = got[:rows], got[rows:]
        turned.append(jnp.concatenate([re * cos[:rows] + im * sin[:rows], im * cos[:rows] - re * sin[:rows]], axis=1))
    high, low = split(jnp.concatenate(turned, axis=0))
    both = mul(jnp.concatenate([high, low], axis=0), d1[0])
    spectra = both[: 2 * rows] + both[2 * rows :] + mul(high, d1[1])

    a_re, a_im = spectra[:64, :128], spectra[:64, 128:]
    b_re, b_im = spectra[rows : rows + 64, :128], spectra[rows : rows + 64, 128:]
    cross_re = a_re * b_re + a_im * b_im
    cross_im = a_re * b_im - a_im * b_re
    first, second = (cross_re, cross_im), (cross_re, -cross_im)

    if chunk == 0:
        def unpack(column, mirror):
            c_re, c_im = column[:, :128], column[:, 128:]
            m_re, m_im = mirror[:, :128], mirror[:, 128:]
            return (c_re + m_re) * 0.5, (c_im + m_im) * 0.5, (c_im - m_im) * 0.5, (m_re - c_re) * 0.5

        a0_re, a0_im, a1_re, a1_im = unpack(spectra[:32], spectra[64:96])
        b0_re, b0_im, b1_re, b1_im = unpack(spectra[96:128], spectra[160:192])
        zero_re, zero_im = a0_re * b0_re + a0_im * b0_im, a0_re * b0_im - a0_im * b0_re
        last_re, last_im = a1_re * b1_re + a1_im * b1_im, a1_re * b1_im - a1_im * b1_re
        lane = lax.broadcasted_iota(jnp.int32, (32, 128), 1)
        packed = jnp.logical_and(lane < ROWS, me_mode == 0)

        def merge(special, plain):
            return jnp.concatenate([jnp.where(packed, special, plain[:32]), plain[32:]], axis=0)

        first = merge(zero_re - last_im, cross_re), merge(zero_im + last_re, cross_im)
        second = merge(zero_re + last_im, cross_re), merge(last_re - zero_im, -cross_im)

    high, low = split(jnp.concatenate([jnp.concatenate(first, axis=1), jnp.concatenate(second, axis=1)], axis=0))
    both = mul(jnp.concatenate([high, low], axis=0), d2[0])
    inner = both[:128] + both[128:] + mul(high, d2[1])
    cos, sin = cos[:64], sin[:64]
    columns = []
    for p in range(2):
        re, im = inner[64 * p : 64 * p + 64, :128], inner[64 * p : 64 * p + 64, 128:]
        columns.append(split(jnp.concatenate([re * cos - im * sin, im * cos + re * sin], axis=0)))
    outer = mul(k2[0], jnp.concatenate([x for pair in columns for x in pair], axis=1))
    outer_low = mul(k2[1], jnp.concatenate([high for high, _ in columns], axis=1))
    for p in range(2):
        got = outer[:, 256 * p : 256 * p + 128] + outer[:, 256 * p + 128 : 256 * p + 256] + outer_low[:, 128 * p : 128 * p + 128]
        got = got.reshape(16, TILE, 128)
        spaced = jnp.stack([got, pltpu.roll(got, TILE // 2, 1)], axis=1)
        send2[chunk, 256 * p : 256 * p + 256, :] = spaced.reshape(256, 128)


def kernel(
    u_hbm, wf_hbm, k1_hbm, d1_hbm, tw_hbm, d2_hbm, k2_hbm, wi_hbm, out_ref,
    u, wf, k1, d1, tw, d2, k2, wi, e_high, e_low, send1, recv1, send2, recv2,
    load_sem, send_sem, recv_sem,
):
    wall, space = lax.axis_index("wall"), lax.axis_index("space")
    pairs = lax.axis_size("wall") // 2
    plane = wall // pairs
    base = lax.rem(wall, pairs)
    y, z = space // 8, lax.rem(space, 8)
    me_mode = y * 16 + plane * 8 + z
    me_row = plane * SPREAD + space

    loads = []
    for i, (src, dst) in enumerate(
        [(u_hbm, u), (wf_hbm, wf), (k1_hbm, k1), (d1_hbm, d1), (tw_hbm, tw), (d2_hbm, d2), (k2_hbm, k2), (wi_hbm, wi)]
    ):
        loads.append(pltpu.make_async_copy(src, dst, load_sem.at[i]))
        loads[-1].start()

    def address(to_plane, to_space):
        return {"device_id": {"wall": base + pairs * to_plane, "space": to_space}, "device_id_type": pl.DeviceIdType.MESH}

    def others(to_z, skip_self=False):
        for dy in (2, 3, 1, 0):
            for flip in (1, 0):
                if not (skip_self and flip == dy == 0):
                    yield lax.rem(plane + flip, 2), lax.rem(y + dy, 4) * 8 + to_z

    def everyone(act):
        @pl.loop(0, 7)
        def _(i):
            act(lax.rem(z + 4 + (1 - 2 * lax.rem(i, 2)) * ((i + 1) // 2), 8))

        act(z, skip_self=True)

    barrier = pltpu.get_barrier_semaphore()

    def greet(to_z, skip_self=False):
        for peer in others(to_z, skip_self):
            pl.semaphore_signal(barrier, inc=1, **address(*peer))

    everyone(greet)

    def tile(ref, index):
        return ref.at[pl.ds(pl.multiple_of(index * TILE, TILE), TILE // 2)]

    def exchange(stage, src, dst, place_there, place_here):
        def send(to_z, skip_self=False):
            for to_plane, to_space in others(to_z, skip_self):
                pltpu.make_async_remote_copy(
                    src_ref=tile(src, place_there(to_plane, to_space)), dst_ref=tile(dst, place_here),
                    send_sem=send_sem.at[stage], recv_sem=recv_sem.at[stage], **address(to_plane, to_space),
                ).start()

        everyone(send)
        pltpu.make_async_copy(tile(src, place_there(plane, space)), tile(dst, place_here), recv_sem.at[stage]).start()

    def wait_tiles(sem, count):
        rows = send1.at[0].at[pl.ds(0, count * TILE // 2)]
        pltpu.make_async_copy(rows, rows, sem).wait()

    def mode_place(of_plane, of_space):
        return (of_space // 8) * 16 + of_plane * 8 + lax.rem(of_space, 8)

    def row_place(of_plane, of_space):
        return of_plane * SPREAD + of_space

    loads[0].wait()
    parts = [u[0, :, 128 * b : 128 * b + 128] for b in range(8)]
    plus = [parts[b] + parts[b + 4] for b in range(4)]
    minus = [parts[b] - parts[b + 4] for b in range(4)]
    even, odd = plus[0] + plus[2], plus[1] + plus[3]
    across, along = (minus[1] - minus[3]) * HALF, (minus[1] + minus[3]) * HALF
    eighths = [
        (even + odd, even - odd),
        (minus[0] + across, -minus[2] - along),
        (plus[0] - plus[2], plus[3] - plus[1]),
        (minus[0] - across, minus[2] - along),
    ]
    for block, (first, second) in enumerate(eighths):
        for half, value in enumerate((first, second)):
            high, low = split(value)
            e_high[block, :, 128 * half : 128 * half + 128] = high
            e_low[block, :, 128 * half : 128 * half + 128] = low

    loads[1].wait()
    nothing = jnp.zeros((ROWS, 256), BF16)
    for block in range(4):
        high, low = e_high[block], e_low[block]
        both = mul_nt(wf[block, 0], jnp.concatenate([high, nothing, low, nothing], axis=0))
        both += mul_nt(wf[block, 1], jnp.concatenate([nothing, high, nothing, low], axis=0))
        got = both[:128, :128] + both[:128, 128:] + both[128:, :128]
        send1[0, 128 * block : 128 * block + 128, :] = got
        got = pltpu.roll(got.reshape(16, TILE, 128), TILE // 2, 1)
        send1[1, 128 * block : 128 * block + 128, :] = got.reshape(128, 128)

    pl.semaphore_wait(barrier, PEERS - 1)
    for chunk in range(2):
        exchange(chunk, send1.at[chunk], recv1.at[chunk], mode_place, me_row)
    for load in loads[2:]:
        load.wait()

    cos, sin = tw[0], tw[1]
    used = lax.broadcasted_iota(jnp.int32, (256, 128), 0) % TILE < TILE // 2
    for chunk in range(2):
        wait_tiles(recv_sem.at[chunk], PEERS)
        stream_chunk(chunk, recv1, send2, k1, d1, d2, k2, cos, sin, used, me_mode)
        exchange(2 + chunk, send2.at[chunk], recv2.at[chunk], row_place, me_mode)
    for chunk in range(2):
        wait_tiles(recv_sem.at[2 + chunk], PEERS)

    upper = lax.broadcasted_iota(jnp.int32, (16, TILE, 128), 1) < TILE // 2
    fields = []
    for block in range(4):
        first, second = [recv2[c, 128 * block : 128 * block + 128, :].reshape(16, TILE, 128) for c in range(2)]
        flat = jnp.where(upper, first, pltpu.roll(second, TILE // 2, 1)).reshape(128, 128).T
        high, low = split(jnp.concatenate([flat[:ROWS], flat[ROWS:]], axis=1))
        both = mul(jnp.concatenate([high, low], axis=0), wi[block, 0])
        fields.append(both[:ROWS] + both[ROWS:] + mul(high, wi[block, 1]))
    (h0, h4), (r1, i1), (r2, i2), (r3, i3) = [(f[:, :128], f[:, 128:]) for f in fields]
    sums, differences = h0 + h4, h0 - h4
    evens = [sums + r2, differences - i2, sums - r2, differences + i2]
    odds = [r1 + r3, (r1 - r3 - i1 - i3) * HALF, i3 - i1, (r3 - r1 - i1 - i3) * HALF]
    for b in range(4):
        out_ref[0, 0, :, 128 * b : 128 * b + 128] = evens[b] + odds[b]
        out_ref[0, 0, :, 128 * b + 512 : 128 * b + 640] = evens[b] - odds[b]

    for stage in range(4):
        wait_tiles(send_sem.at[stage], PEERS - 1)


def local(velocity):
    tables = [
        span_forward_tables(), stream_outer_forward(), stream_inner(-1.0), twist_tables(),
        stream_inner(1.0), stream_outer_inverse(), span_inverse_tables(),
    ]
    tables = [jnp.asarray(t) for t in tables]
    messages = pltpu.VMEM((2, PEERS * TILE, 128), F32)
    return pl.pallas_call(
        kernel,
        out_shape=jax.ShapeDtypeStruct((1, 1, ROWS, NZ), F32),
        in_specs=[pl.BlockSpec(memory_space=pl.ANY)] * 8,
        out_specs=pl.BlockSpec(memory_space=pltpu.VMEM),
        scratch_shapes=[pltpu.VMEM(velocity.shape, F32)]
        + [pltpu.VMEM(t.shape, t.dtype) for t in tables]
        + [pltpu.VMEM((4, ROWS, 256), BF16)] * 2
        + [messages] * 4
        + [pltpu.SemaphoreType.DMA((8,)), pltpu.SemaphoreType.DMA((4,)), pltpu.SemaphoreType.DMA((4,))],
        compiler_params=pltpu.CompilerParams(
            collective_id=0, has_side_effects=True, vmem_limit_bytes=56 * 1024 * 1024
        ),
    )(velocity, *tables)


def solution(mesh):
    return jax.shard_map(
        local, mesh=mesh, in_specs=(P("wall", "space", None),), out_specs=P("wall", None, "space", None), check_vma=False
    )
```

time: 46.5 us -> 36.5 us (0.78)
  local copies, waits for them, and re-layouts: 8.84 us -> 1.67 us
  Pallas kernels: 37.3 us -> 34.6 us
    unnamed x17 -> x1, local copies, waits for them, and re-layouts: 8.84 us -> 1.67 us
    pallas_call x1, Pallas kernels: 37.3 us -> 34.6 us  [local(): pl.pallas_call(kernel, out_shape=jax.ShapeDtypeStruct((1, 1, ROWS, NZ), F...]
where the time goes in v2:
time: 36.5 us; the launch traced here: 36.3 us
  Pallas kernels  34.6 us (95%)
  local copies, waits for them, and re-layouts  1.67 us (5%)
    pallas_call x1, Pallas kernels, local(): pl.pallas_call(kernel, out_shape=jax.ShapeDtypeStruct((1, 1, ROWS, NZ), F...  34.6 us
    unnamed x1, local copies, waits for them, and re-layouts  1.67 us

profile of v2, /device:TPU:56, one launch (start us, length us, event | category | flops | bytes accessed | tf_op | source)
XLA Modules:
  0.0 36.3 jit_solution(900854559930570333)
XLA Ops:
  0.0 34.6 %shard_map.82 = f32[1,1,64,1024]{3,2,1,0:T(8,128)} custom-call(f32[1,64,1024]{2,1,0:T(8,128)} %u_hbm.1, bf16[4,2,256,256]{3,2,1,0:T(8,128)(2,1)} %constant.14.clone.wf_hbm, bf16[2,192,256]{2,1,0:T(8,128)(2,1)} %constant.15.clone.k1_hbm, bf16[2,256,256]{2,1,0:T(8,128)(2,1)} %constant.16.clone.d1_hbm, f32[2,96,128]{2,1,0:T(8,128)} %constant.17.clone.tw_hbm, ...), custom_call_target="tpu_custom_call" | custom-call | tf_op jit(solution)/shard_map/pallas_call | solution.py:345
  34.6 1.7 %copy.10 = f32[1,1,64,1024]{3,2,1,0:T(8,128)} copy(f32[1,1,64,1024]{3,2,1,0:T(8,128)} %shard_map.82) | data formatting | bytes 524288

commit v3 on v2

v3 whole, which is shorter than its diff:
```python
import math

import jax
import jax.numpy as jnp
import ml_dtypes
import numpy as np
from jax import lax
from jax.experimental import pallas as pl
from jax.experimental.pallas import tpu as pltpu
from jax.sharding import PartitionSpec as P

F32 = jnp.float32
BF16 = jnp.bfloat16
HALF = math.sqrt(0.5)

NX, NZ = 2048, 1024
SPREAD, ROWS = 32, 64
PEERS = 2 * SPREAD
TILE = 8
CHUNKS = 2
MESSAGE = TILE // CHUNKS
COLUMNS = MESSAGE // 2
RUN = COLUMNS * SPREAD


def split_table(table):
    high = table.astype(ml_dtypes.bfloat16)
    low = (table - high.astype(np.float64)).astype(ml_dtypes.bfloat16)
    return high, low


def mode_of(block, n):
    if block:
        return 8 * n + block
    return np.where(n < 64, 8 * n, 8 * (n - 64) + 4)


def slots():
    kb, dev, chunk, part, ka = np.meshgrid(*map(np.arange, (2, 16, CHUNKS, 2, COLUMNS)), indexing="ij")
    return dev * 8 + (chunk * COLUMNS + ka) * 2 + kb, part


def span_forward_tables():
    n, part = slots()
    n, part = n[..., None], part[..., None]
    zi = np.arange(128)
    out = np.zeros((4, 2, 128, 256))
    for block in range(4):
        angle = 2 * np.pi * (mode_of(block, n) * zi % NZ) / NZ
        cos, sin = np.cos(angle), np.sin(angle)
        from_re = np.where(part == 0, cos, -sin)
        from_im = np.where(part == 0, sin, cos)
        if block == 0:
            alternate = np.where(zi % 2 == 0, 1.0, -1.0)
            from_re = np.where((n == 0) & (part == 1), alternate, from_re)
            first = np.where(n < 64, from_re, 0.0)
            second = np.where(n < 64, 0.0, from_re)
        else:
            first, second = from_re, from_im
        out[block] = np.concatenate([first, second], axis=-1).reshape(2, 128, 256)
    high, low = split_table(out)
    return np.concatenate([high, low], axis=2)


def span_inverse_tables():
    n, part = slots()
    n, part = n[..., None], part[..., None]
    zi = np.arange(128)
    scale = (NX * NZ) ** -1.5
    out = np.zeros((4, 256, 256))
    for block in range(4):
        angle = 2 * np.pi * (mode_of(block, n) * zi % NZ) / NZ
        cos, sin = np.cos(angle), np.sin(angle)
        to_re = 2 * np.where(part == 0, cos, -sin)
        to_im = 2 * np.where(part == 0, sin, cos)
        if block == 0:
            alternate = np.where(zi % 2 == 0, 1.0, -1.0)
            to_re = np.where(n == 0, np.where(part == 0, 1.0, alternate), to_re)
            first = np.where(n < 64, to_re, 0.0)
            second = np.where(n < 64, 0.0, to_re)
        else:
            first, second = to_re, to_im
        out[block] = np.concatenate([first, second], axis=-1).reshape(256, 256) * scale
    high, low = split_table(out)
    return np.stack([high, low], axis=1)


def stream_outer_forward():
    out = np.zeros((2, RUN, SPREAD, TILE))
    mirror = np.zeros((2, SPREAD, SPREAD, TILE))
    t, s = np.arange(SPREAD)[:, None], np.arange(SPREAD)[None, :]
    cos, sin = np.cos(2 * np.pi * (t * s % 32) / 32), np.sin(2 * np.pi * (t * s % 32) / 32)
    for ka in range(COLUMNS):
        rows = slice(32 * ka, 32 * ka + 32)
        out[0, rows, :, ka] = cos
        out[0, rows, :, COLUMNS + ka] = sin
        out[1, rows, :, ka] = -sin
        out[1, rows, :, COLUMNS + ka] = cos
    mirror[0, :, :, 0] = cos
    mirror[0, :, :, COLUMNS] = -sin
    mirror[1, :, :, 0] = -sin
    mirror[1, :, :, COLUMNS] = -cos
    out = np.concatenate([out.reshape(2 * RUN, 256), mirror.reshape(64, 256)])
    return np.concatenate(split_table(out))


def stream_outer_inverse():
    out = np.zeros((SPREAD, 2, COLUMNS, 2, COLUMNS, SPREAD))
    s, t = np.arange(SPREAD)[:, None], np.arange(SPREAD)[None, :]
    cos, sin = np.cos(2 * np.pi * (t * s % 32) / 32), np.sin(2 * np.pi * (t * s % 32) / 32)
    for ka in range(COLUMNS):
        out[:, 0, ka, 0, ka] = cos
        out[:, 0, ka, 1, ka] = -sin
        out[:, 1, ka, 0, ka] = sin
        out[:, 1, ka, 1, ka] = cos
    high, low = split_table(out.reshape(2 * RUN, 2 * RUN))
    pad = np.zeros((2 * RUN, 128 - 2 * RUN), high.dtype)
    return np.concatenate([high, pad, low, pad], axis=1)


def stream_inner(sign):
    out = np.zeros((2, 2, ROWS, 2, 2, ROWS))
    r, m = np.arange(ROWS)[:, None], np.arange(ROWS)[None, :]
    cos, sin = np.cos(2 * np.pi * (r * m % 64) / 64), sign * np.sin(2 * np.pi * (r * m % 64) / 64)
    for kb in range(2):
        out[0, kb, :, 0, kb] = cos
        out[1, kb, :, 0, kb] = -sin
        out[0, kb, :, 1, kb] = sin
        out[1, kb, :, 1, kb] = cos
    return np.concatenate(split_table(out.reshape(256, 256)))


def twist_tables():
    angle = 2 * np.pi * np.outer(np.arange(SPREAD), np.tile(np.arange(ROWS), 2)) / NX
    return np.concatenate(split_table(np.concatenate([np.cos(angle), np.sin(angle)], axis=1)))


TABLES = {
    "span_forward": span_forward_tables().reshape(-1, 256),
    "outer_forward": stream_outer_forward(),
    "inner_forward": stream_inner(-1.0),
    "twist": twist_tables(),
    "inner_inverse": stream_inner(1.0),
    "outer_inverse": stream_outer_inverse(),
    "span_inverse": span_inverse_tables().reshape(-1, 256),
}
STARTS = dict(zip(TABLES, np.cumsum([0] + [t.shape[0] for t in TABLES.values()]).tolist()))
TABLE_ROWS = sum(t.shape[0] for t in TABLES.values())


def table_rows(tables, name, first, count):
    return tables[STARTS[name] + first : STARTS[name] + first + count, :]


def split(x):
    high = x.astype(BF16)
    return high, (x - high.astype(F32)).astype(BF16)


def mul(a, b):
    return jnp.dot(a, b, preferred_element_type=F32)


def mul_nt(a, b):
    return lax.dot_general(a, b, (((1,), (1,)), ((), ())), preferred_element_type=F32)


def stream_chunk(chunk, recv1, send2, tables, me_mode):
    used = lax.broadcasted_iota(jnp.int32, (256, 128), 0) % TILE < MESSAGE
    halves = [split(jnp.where(used, recv1[chunk, 256 * p : 256 * p + 256, :], 0.0)) for p in range(2)]
    extra = 64 if chunk == 0 else 0
    rows = RUN + extra // 2
    high, low = [table_rows(tables, "outer_forward", first, 2 * RUN + extra) for first in (0, 2 * RUN + 64)]
    outer = mul(high, jnp.concatenate([x for pair in halves for x in pair], axis=1))
    outer_low = mul(low, jnp.concatenate([x for x, _ in halves], axis=1))
    twist = table_rows(tables, "twist", 0, 32).astype(F32) + table_rows(tables, "twist", 32, 32).astype(F32)
    cos = jnp.concatenate([twist[:, :128]] * (rows // 32), axis=0)
    sin = jnp.concatenate([twist[:, 128:]] * (rows // 32), axis=0)
    turned = []
    for p in range(2):
        got = outer[:, 256 * p : 256 * p + 128] + outer[:, 256 * p + 128 : 256 * p + 256] + outer_low[:, 128 * p : 128 * p + 128]
        re, im = got[:RUN], got[RUN : 2 * RUN]
        if extra:
            re = jnp.concatenate([re, got[2 * RUN : 2 * RUN + 32]], axis=0)
            im = jnp.concatenate([im, got[2 * RUN + 32 :]], axis=0)
        turned.append(jnp.concatenate([re * cos + im * sin, im * cos - re * sin], axis=1))
    high, low = split(jnp.concatenate(turned, axis=0))
    both = mul(jnp.concatenate([high, low], axis=0), table_rows(tables, "inner_forward", 0, 256))
    spectra = both[: 2 * rows] + both[2 * rows :] + mul(high, table_rows(tables, "inner_forward", 256, 256))

    a_re, a_im = spectra[:RUN, :128], spectra[:RUN, 128:]
    b_re, b_im = spectra[rows : rows + RUN, :128], spectra[rows : rows + RUN, 128:]
    cross_re = a_re * b_re + a_im * b_im
    cross_im = a_re * b_im - a_im * b_re
    first, second = (cross_re, cross_im), (cross_re, -cross_im)

    if chunk == 0:
        def unpack(column, mirror):
            c_re, c_im = column[:, :128], column[:, 128:]
            m_re, m_im = mirror[:, :128], mirror[:, 128:]
            return (c_re + m_re) * 0.5, (c_im + m_im) * 0.5, (c_im - m_im) * 0.5, (m_re - c_re) * 0.5

        a0_re, a0_im, a1_re, a1_im = unpack(spectra[:32], spectra[RUN:rows])
        b0_re, b0_im, b1_re, b1_im = unpack(spectra[rows : rows + 32], spectra[rows + RUN :])
        zero_re, zero_im = a0_re * b0_re + a0_im * b0_im, a0_re * b0_im - a0_im * b0_re
        last_re, last_im = a1_re * b1_re + a1_im * b1_im, a1_re * b1_im - a1_im * b1_re
        lane = lax.broadcasted_iota(jnp.int32, (32, 128), 1)
        packed = jnp.logical_and(lane < ROWS, me_mode == 0)

        def merge(special, plain):
            head = jnp.where(packed, special, plain[:32])
            return head if RUN == 32 else jnp.concatenate([head, plain[32:]], axis=0)

        first = merge(zero_re - last_im, cross_re), merge(zero_im + last_re, cross_im)
        second = merge(zero_re + last_im, cross_re), merge(last_re - zero_im, -cross_im)

    high, low = split(jnp.concatenate([jnp.concatenate(first, axis=1), jnp.concatenate(second, axis=1)], axis=0))
    both = mul(jnp.concatenate([high, low], axis=0), table_rows(tables, "inner_inverse", 0, 256))
    inner = both[: 2 * RUN] + both[2 * RUN :] + mul(high, table_rows(tables, "inner_inverse", 256, 256))
    cos, sin = cos[:RUN], sin[:RUN]
    columns = []
    for p in range(2):
        re, im = inner[RUN * p : RUN * p + RUN, :128], inner[RUN * p : RUN * p + RUN, 128:]
        columns.append(split(jnp.concatenate([re * cos - im * sin, im * cos + re * sin], axis=0)))
    outer_table = table_rows(tables, "outer_inverse", 0, 2 * RUN)
    outer = mul(outer_table[:, : 2 * RUN], jnp.concatenate([x for pair in columns for x in pair], axis=1))
    outer_low = mul(outer_table[:, 128 : 128 + 2 * RUN], jnp.concatenate([x for x, _ in columns], axis=1))
    for p in range(2):
        got = outer[:, 256 * p : 256 * p + 128] + outer[:, 256 * p + 128 : 256 * p + 256] + outer_low[:, 128 * p : 128 * p + 128]
        got = got.reshape(SPREAD // CHUNKS, TILE, 128)
        spaced = jnp.stack([got] + [pltpu.roll(got, TILE - MESSAGE * i, 1) for i in range(1, CHUNKS)], axis=1)
        send2[chunk, 256 * p : 256 * p + 256, :] = spaced.reshape(256, 128)


def kernel(
    u_hbm, tables_hbm, out_ref, u, tables, e_high, e_low, send1, recv1, send2, recv2,
    load_sem, send_sem, recv_sem,
):
    wall, space = lax.axis_index("wall"), lax.axis_index("space")
    pairs = lax.axis_size("wall") // 2
    plane = wall // pairs
    base = lax.rem(wall, pairs)
    y, z = space // 8, lax.rem(space, 8)
    me_mode = y * 16 + plane * 8 + z
    me_row = plane * SPREAD + space

    first = STARTS["outer_forward"]
    loads = [
        pltpu.make_async_copy(u_hbm, u, load_sem.at[0]),
        pltpu.make_async_copy(tables_hbm.at[pl.ds(0, first)], tables.at[pl.ds(0, first)], load_sem.at[1]),
        pltpu.make_async_copy(
            tables_hbm.at[pl.ds(first, TABLE_ROWS - first)], tables.at[pl.ds(first, TABLE_ROWS - first)], load_sem.at[2]
        ),
    ]
    for load in loads:
        load.start()

    def address(to_plane, to_space):
        return {"device_id": {"wall": base + pairs * to_plane, "space": to_space}, "device_id_type": pl.DeviceIdType.MESH}

    def others(to_z, skip_self=False):
        for dy in (2, 3, 1, 0):
            for flip in (1, 0):
                if not (skip_self and flip == dy == 0):
                    yield lax.rem(plane + flip, 2), lax.rem(y + dy, 4) * 8 + to_z

    def everyone(act):
        @pl.loop(0, 7)
        def _(i):
            act(lax.rem(z + 4 + (1 - 2 * lax.rem(i, 2)) * ((i + 1) // 2), 8))

        act(z, skip_self=True)

    barrier = pltpu.get_barrier_semaphore()

    def greet(to_z, skip_self=False):
        for peer in others(to_z, skip_self):
            pl.semaphore_signal(barrier, inc=1, **address(*peer))

    everyone(greet)

    def tile(ref, index):
        return ref.at[pl.ds(pl.multiple_of(index * TILE, TILE), MESSAGE)]

    def exchange(stage, src, dst, place_there, place_here):
        def send(to_z, skip_self=False):
            for to_plane, to_space in others(to_z, skip_self):
                pltpu.make_async_remote_copy(
                    src_ref=tile(src, place_there(to_plane, to_space)), dst_ref=tile(dst, place_here),
                    send_sem=send_sem.at[stage], recv_sem=recv_sem.at[stage], **address(to_plane, to_space),
                ).start()

        everyone(send)
        pltpu.make_async_copy(tile(src, place_there(plane, space)), tile(dst, place_here), recv_sem.at[stage]).start()

    def wait_tiles(sem, count):
        rows = send1.at[0].at[pl.ds(0, count * MESSAGE)]
        pltpu.make_async_copy(rows, rows, sem).wait()

    def mode_place(of_plane, of_space):
        return (of_space // 8) * 16 + of_plane * 8 + lax.rem(of_space, 8)

    def row_place(of_plane, of_space):
        return of_plane * SPREAD + of_space

    loads[0].wait()
    parts = [u[0, :, 128 * b : 128 * b + 128] for b in range(8)]
    plus = [parts[b] + parts[b + 4] for b in range(4)]
    minus = [parts[b] - parts[b + 4] for b in range(4)]
    even, odd = plus[0] + plus[2], plus[1] + plus[3]
    across, along = (minus[1] - minus[3]) * HALF, (minus[1] + minus[3]) * HALF
    eighths = [
        (even + odd, even - odd),
        (minus[0] + across, -minus[2] - along),
        (plus[0] - plus[2], plus[3] - plus[1]),
        (minus[0] - across, minus[2] - along),
    ]
    for block, (first, second) in enumerate(eighths):
        for half, value in enumerate((first, second)):
            high, low = split(value)
            e_high[block, :, 128 * half : 128 * half + 128] = high
            e_low[block, :, 128 * half : 128 * half + 128] = low

    loads[1].wait()
    nothing = jnp.zeros((ROWS, 256), BF16)
    for block in range(4):
        high, low = e_high[block], e_low[block]
        first, second = [table_rows(tables, "span_forward", 512 * block + 256 * kb, 256) for kb in range(2)]
        both = mul_nt(first, jnp.concatenate([high, nothing, low, nothing], axis=0))
        both += mul_nt(second, jnp.concatenate([nothing, high, nothing, low], axis=0))
        got = both[:128, :128] + both[:128, 128:] + both[128:, :128]
        got = got.reshape(16, TILE, 128)
        for chunk in range(CHUNKS):
            turned = pltpu.roll(got, TILE - MESSAGE * chunk, 1) if chunk else got
            send1[chunk, 128 * block : 128 * block + 128, :] = turned.reshape(128, 128)

    pl.semaphore_wait(barrier, PEERS - 1)
    for chunk in range(CHUNKS):
        exchange(chunk, send1.at[chunk], recv1.at[chunk], mode_place, me_row)
    loads[2].wait()
    for chunk in range(CHUNKS):
        wait_tiles(recv_sem.at[chunk], PEERS)
        stream_chunk(chunk, recv1, send2, tables, me_mode)
        exchange(CHUNKS + chunk, send2.at[chunk], recv2.at[chunk], row_place, me_mode)
    for chunk in range(CHUNKS):
        wait_tiles(recv_sem.at[CHUNKS + chunk], PEERS)

    place = lax.broadcasted_iota(jnp.int32, (16, TILE, 128), 1) // MESSAGE
    fields = []
    for block in range(4):
        flat = recv2[0, 128 * block : 128 * block + 128, :].reshape(16, TILE, 128)
        for chunk in range(1, CHUNKS):
            got = recv2[chunk, 128 * block : 128 * block + 128, :].reshape(16, TILE, 128)
            flat = jnp.where(place == chunk, pltpu.roll(got, MESSAGE * chunk, 1), flat)
        flat = flat.reshape(128, 128).T
        high, low = split(jnp.concatenate([flat[:ROWS], flat[ROWS:]], axis=1))
        first, second = [table_rows(tables, "span_inverse", 512 * block + 256 * i, 256) for i in range(2)]
        both = mul(jnp.concatenate([high, low], axis=0), first)
        fields.append(both[:ROWS] + both[ROWS:] + mul(high, second))
    (h0, h4), (r1, i1), (r2, i2), (r3, i3) = [(f[:, :128], f[:, 128:]) for f in fields]
    sums, differences = h0 + h4, h0 - h4
    evens = [sums + r2, differences - i2, sums - r2, differences + i2]
    odds = [r1 + r3, (r1 - r3 - i1 - i3) * HALF, i3 - i1, (r3 - r1 - i1 - i3) * HALF]
    for b in range(4):
        out_ref[0, 0, :, 128 * b : 128 * b + 128] = evens[b] + odds[b]
        out_ref[0, 0, :, 128 * b + 512 : 128 * b + 640] = evens[b] - odds[b]

    for stage in range(2 * CHUNKS):
        wait_tiles(send_sem.at[stage], PEERS - 1)


def local(velocity):
    tables = jnp.asarray(np.concatenate(list(TABLES.values())))
    messages = pltpu.VMEM((CHUNKS, PEERS * TILE, 128), F32)
    return pl.pallas_call(
        kernel,
        out_shape=jax.ShapeDtypeStruct((1, 1, ROWS, NZ), F32),
        in_specs=[pl.BlockSpec(memory_space=pl.ANY)] * 2,
        out_specs=pl.BlockSpec(memory_space=pltpu.VMEM),
        scratch_shapes=[pltpu.VMEM(velocity.shape, F32), pltpu.VMEM(tables.shape, tables.dtype)]
        + [pltpu.VMEM((4, ROWS, 256), BF16)] * 2
        + [messages] * 4
        + [pltpu.SemaphoreType.DMA((n,)) for n in (3, 2 * CHUNKS, 2 * CHUNKS)],
        compiler_params=pltpu.CompilerParams(
            collective_id=0, has_side_effects=True, vmem_limit_bytes=107 * 512 * 1024
        ),
    )(velocity, tables)


def solution(mesh):
    return jax.shard_map(
        local, mesh=mesh, in_specs=(P("wall", "space", None),), out_specs=P("wall", None, "space", None), check_vma=False
    )
```

time: 36.5 us -> 34.7 us (0.951)
  local copies, waits for them, and re-layouts: 1.67 us -> 0.71 us
  Pallas kernels: 34.6 us -> 33.9 us
    unnamed x1, local copies, waits for them, and re-layouts: 1.67 us -> 0.71 us
    pallas_call x1, Pallas kernels: 34.6 us -> 33.9 us  [local(): pl.pallas_call(kernel, out_shape=jax.ShapeDtypeStruct((1, 1, ROWS, NZ), F...]
where the time goes in v3:
time: 34.7 us; the launch traced here: 34.6 us
  Pallas kernels  33.9 us (98%)
  local copies, waits for them, and re-layouts  0.71 us (2%)
    pallas_call x1, Pallas kernels, local(): pl.pallas_call(kernel, out_shape=jax.ShapeDtypeStruct((1, 1, ROWS, NZ), F...  33.9 us
    unnamed x1, local copies, waits for them, and re-layouts  0.71 us

profile of v3, /device:TPU:56, one launch (start us, length us, event | category | flops | bytes accessed | tf_op | source)
XLA Modules:
  0.0 34.6 jit_solution(15428800563017665239)
XLA Ops:
  0.0 33.9 %shard_map.28 = f32[1,1,64,1024]{3,2,1,0:T(8,128)S(1)} custom-call(f32[1,64,1024]{2,1,0:T(8,128)} %u_hbm.1, bf16[5696,256]{1,0:T(8,128)(2,1)} %constant.2.clone.tables_hbm), custom_call_target="tpu_custom_call" | custom-call | tf_op jit(solution)/shard_map/pallas_call | solution.py:375
  33.9 0.7 %copy.4 = f32[1,1,64,1024]{3,2,1,0:T(8,128)} copy(f32[1,1,64,1024]{3,2,1,0:T(8,128)S(1)} %shard_map.28) | data formatting | bytes 524288

commit v4 on v3

--- a/solution.py
+++ b/solution.py
@@ -244,6 +244,28 @@
     me_mode = y * 16 + plane * 8 + z
     me_row = plane * SPREAD + space
 
+    def address(to_plane, to_space):
+        return {"device_id": {"wall": base + pairs * to_plane, "space": to_space}, "device_id_type": pl.DeviceIdType.MESH}
+
+    def everyone(act):
+        def row(flip, dz, steps):
+            for dy in steps:
+                act(lax.rem(plane + flip, 2), lax.rem(y + dy, 4) * 8 + lax.rem(z + dz, 8))
+
+        for flip in (1, 0):
+            @pl.loop(0, 7)
+            def _(i):
+                row(flip, 4 + (1 - 2 * lax.rem(i, 2)) * ((i + 1) // 2), (1, 3, 2, 0))
+
+            row(flip, 0, (1, 3, 2, 0) if flip else (1, 3, 2))
+
+    barrier = pltpu.get_barrier_semaphore()
+
+    def greet(to_plane, to_space):
+        pl.semaphore_signal(barrier, inc=1, **address(to_plane, to_space))
+
+    everyone(greet)
+
     first = STARTS["outer_forward"]
     loads = [
         pltpu.make_async_copy(u_hbm, u, load_sem.at[0]),
@@ -255,40 +277,15 @@
     for load in loads:
         load.start()
 
-    def address(to_plane, to_space):
-        return {"device_id": {"wall": base + pairs * to_plane, "space": to_space}, "device_id_type": pl.DeviceIdType.MESH}
-
-    def others(to_z, skip_self=False):
-        for dy in (2, 3, 1, 0):
-            for flip in (1, 0):
-                if not (skip_self and flip == dy == 0):
-                    yield lax.rem(plane + flip, 2), lax.rem(y + dy, 4) * 8 + to_z
-
-    def everyone(act):
-        @pl.loop(0, 7)
-        def _(i):
-            act(lax.rem(z + 4 + (1 - 2 * lax.rem(i, 2)) * ((i + 1) // 2), 8))
-
-        act(z, skip_self=True)
-
-    barrier = pltpu.get_barrier_semaphore()
-
-    def greet(to_z, skip_self=False):
-        for peer in others(to_z, skip_self):
-            pl.semaphore_signal(barrier, inc=1, **address(*peer))
-
-    everyone(greet)
-
     def tile(ref, index):
         return ref.at[pl.ds(pl.multiple_of(index * TILE, TILE), MESSAGE)]
 
     def exchange(stage, src, dst, place_there, place_here):
-        def send(to_z, skip_self=False):
-            for to_plane, to_space in others(to_z, skip_self):
-                pltpu.make_async_remote_copy(
-                    src_ref=tile(src, place_there(to_plane, to_space)), dst_ref=tile(dst, place_here),
-                    send_sem=send_sem.at[stage], recv_sem=recv_sem.at[stage], **address(to_plane, to_space),
-                ).start()
+        def send(to_plane, to_space):
+            pltpu.make_async_remote_copy(
+                src_ref=tile(src, place_there(to_plane, to_space)), dst_ref=tile(dst, place_here),
+                send_sem=send_sem.at[stage], recv_sem=recv_sem.at[stage], **address(to_plane, to_space),
+            ).start()
 
         everyone(send)
         pltpu.make_async_copy(tile(src, place_there(plane, space)), tile(dst, place_here), recv_sem.at[stage]).start()

time: 34.7 us -> 34.2 us (0.986)
  Pallas kernels: 33.9 us -> 33.4 us
    pallas_call x1, Pallas kernels: 33.9 us -> 33.4 us  [local(): pl.pallas_call(kernel, out_shape=jax.ShapeDtypeStruct((1, 1, ROWS, NZ), F...]
where the time goes in v4:
time: 34.2 us; the launch traced here: 34.1 us
  Pallas kernels  33.4 us (98%)
  local copies, waits for them, and re-layouts  0.71 us (2%)
    pallas_call x1, Pallas kernels, local(): pl.pallas_call(kernel, out_shape=jax.ShapeDtypeStruct((1, 1, ROWS, NZ), F...  33.4 us
    unnamed x1, local copies, waits for them, and re-layouts  0.71 us

profile of v4, /device:TPU:56, one launch (start us, length us, event | category | flops | bytes accessed | tf_op | source)
XLA Modules:
  0.0 34.1 jit_solution(6221188125533889739)
XLA Ops:
  0.0 33.4 %shard_map.28 = f32[1,1,64,1024]{3,2,1,0:T(8,128)S(1)} custom-call(f32[1,64,1024]{2,1,0:T(8,128)} %u_hbm.1, bf16[5696,256]{1,0:T(8,128)(2,1)} %constant.2.clone.tables_hbm), custom_call_target="tpu_custom_call" | custom-call | tf_op jit(solution)/shard_map/pallas_call | solution.py:372
  33.4 0.7 %copy.4 = f32[1,1,64,1024]{3,2,1,0:T(8,128)} copy(f32[1,1,64,1024]{3,2,1,0:T(8,128)S(1)} %shard_map.28) | data formatting | bytes 524288

commit v5 on v4

--- a/solution.py
+++ b/solution.py
@@ -248,16 +248,19 @@
         return {"device_id": {"wall": base + pairs * to_plane, "space": to_space}, "device_id_type": pl.DeviceIdType.MESH}
 
     def everyone(act):
-        def row(flip, dz, steps):
+        def row(flip, steps, *shifts):
             for dy in steps:
-                act(lax.rem(plane + flip, 2), lax.rem(y + dy, 4) * 8 + lax.rem(z + dz, 8))
+                for dz in shifts:
+                    act(lax.rem(plane + flip, 2), lax.rem(y + dy, 4) * 8 + lax.rem(z + dz, 8))
 
         for flip in (1, 0):
-            @pl.loop(0, 7)
+            row(flip, (1, 3, 2, 0), 4)
+
+            @pl.loop(1, 4)
             def _(i):
-                row(flip, 4 + (1 - 2 * lax.rem(i, 2)) * ((i + 1) // 2), (1, 3, 2, 0))
-
-            row(flip, 0, (1, 3, 2, 0) if flip else (1, 3, 2))
+                row(flip, (1, 3, 2, 0), 4 - i, 4 + i)
+
+            row(flip, (1, 3, 2, 0) if flip else (1, 3, 2), 0)
 
     barrier = pltpu.get_barrier_semaphore()
 
@@ -320,16 +323,17 @@
 
     loads[1].wait()
     nothing = jnp.zeros((ROWS, 256), BF16)
-    for block in range(4):
+    @pl.loop(0, 4)
+    def _(block):
         high, low = e_high[block], e_low[block]
-        first, second = [table_rows(tables, "span_forward", 512 * block + 256 * kb, 256) for kb in range(2)]
+        first, second = [tables[pl.ds(pl.multiple_of(512 * block + 256 * kb, 256), 256), :] for kb in range(2)]
         both = mul_nt(first, jnp.concatenate([high, nothing, low, nothing], axis=0))
         both += mul_nt(second, jnp.concatenate([nothing, high, nothing, low], axis=0))
         got = both[:128, :128] + both[:128, 128:] + both[128:, :128]
         got = got.reshape(16, TILE, 128)
         for chunk in range(CHUNKS):
             turned = pltpu.roll(got, TILE - MESSAGE * chunk, 1) if chunk else got
-            send1[chunk, 128 * block : 128 * block + 128, :] = turned.reshape(128, 128)
+            send1[chunk, pl.ds(pl.multiple_of(128 * block, 128), 128), :] = turned.reshape(128, 128)
 
     pl.semaphore_wait(barrier, PEERS - 1)
     for chunk in range(CHUNKS):

time: 34.2 us -> 34.1 us (level)
  no operation moved by 1% of the time
where the time goes in v5:
time: 34.1 us; the launch traced here: 34 us
  Pallas kernels  33.3 us (98%)
  local copies, waits for them, and re-layouts  0.71 us (2%)
    pallas_call x1, Pallas kernels, local(): pl.pallas_call(kernel, out_shape=jax.ShapeDtypeStruct((1, 1, ROWS, NZ), F...  33.3 us
    unnamed x1, local copies, waits for them, and re-layouts  0.71 us

profile of v5, /device:TPU:56, one launch (start us, length us, event | category | flops | bytes accessed | tf_op | source)
XLA Modules:
  0.0 34.0 jit_solution(16020415914482583007)
XLA Ops:
  0.0 33.3 %shard_map.28 = f32[1,1,64,1024]{3,2,1,0:T(8,128)S(1)} custom-call(f32[1,64,1024]{2,1,0:T(8,128)} %u_hbm.1, bf16[5696,256]{1,0:T(8,128)(2,1)} %constant.2.clone.tables_hbm), custom_call_target="tpu_custom_call" | custom-call | tf_op jit(solution)/shard_map/pallas_call | solution.py:376
  33.3 0.7 %copy.4 = f32[1,1,64,1024]{3,2,1,0:T(8,128)} copy(f32[1,1,64,1024]{3,2,1,0:T(8,128)S(1)} %shard_map.28) | data formatting | bytes 524288

commit v6 on v5

--- a/solution.py
+++ b/solution.py
@@ -343,6 +343,8 @@
         wait_tiles(recv_sem.at[chunk], PEERS)
         stream_chunk(chunk, recv1, send2, tables, me_mode)
         exchange(CHUNKS + chunk, send2.at[chunk], recv2.at[chunk], row_place, me_mode)
+    for stage in range(2 * CHUNKS):
+        wait_tiles(send_sem.at[stage], PEERS - 1)
     for chunk in range(CHUNKS):
         wait_tiles(recv_sem.at[CHUNKS + chunk], PEERS)
 
@@ -366,9 +368,6 @@
         out_ref[0, 0, :, 128 * b : 128 * b + 128] = evens[b] + odds[b]
         out_ref[0, 0, :, 128 * b + 512 : 128 * b + 640] = evens[b] - odds[b]
 
-    for stage in range(2 * CHUNKS):
-        wait_tiles(send_sem.at[stage], PEERS - 1)
-
 
 def local(velocity):
     tables = jnp.asarray(np.concatenate(list(TABLES.values())))

time: 34.1 us -> 34.1 us (level)
  no operation moved by 1% of the time
where the time goes in v6:
time: 34.1 us; the launch traced here: 34 us
  Pallas kernels  33.3 us (98%)
  local copies, waits for them, and re-layouts  0.71 us (2%)
    pallas_call x1, Pallas kernels, local(): pl.pallas_call(kernel, out_shape=jax.ShapeDtypeStruct((1, 1, ROWS, NZ), F...  33.3 us
    unnamed x1, local copies, waits for them, and re-layouts  0.71 us

profile of v6, /device:TPU:56, one launch (start us, length us, event | category | flops | bytes accessed | tf_op | source)
XLA Modules:
  0.0 34.0 jit_solution(7218228040661048780)
XLA Ops:
  0.0 33.3 %shard_map.28 = f32[1,1,64,1024]{3,2,1,0:T(8,128)S(1)} custom-call(f32[1,64,1024]{2,1,0:T(8,128)} %u_hbm.1, bf16[5696,256]{1,0:T(8,128)(2,1)} %constant.2.clone.tables_hbm), custom_call_target="tpu_custom_call" | custom-call | tf_op jit(solution)/shard_map/pallas_call | solution.py:375
  33.3 0.7 %copy.4 = f32[1,1,64,1024]{3,2,1,0:T(8,128)} copy(f32[1,1,64,1024]{3,2,1,0:T(8,128)S(1)} %shard_map.28) | data formatting | bytes 524288
